TPU v7x, 32 devices: a whole 2x2x4 slice. The times are simulated.
32 devices in a mesh: dp: 4 (over y, core), mem: 8 (over z, x).
Axes of the slice: x: 2, y: 2, z: 4, core: 2. Of those that a mesh axis runs over, the one named last changes fastest.
Arguments:
- slot_weight: bfloat16 [4096, 32], P(('dp', 'mem')), may hold values from -1.1953125 to 1.1953125
- slot_pos: int32 [4096, 32], P(('dp', 'mem')), may hold values from 0 to 255, as said below
- touched: int32 [32, 8, 32], P(('dp', 'mem')), may hold values from 0 to 255, as said below
- values: bfloat16 [2048, 4096], P('mem'), may hold values from -6 to 6
- cotangent: bfloat16 [4096, 4096], P(('dp', 'mem')), may hold values from -6 to 6
Outputs:
- memory_out: bfloat16 [4096, 4096], P(('dp', 'mem'))
- weight_grad: float32 [4096, 32], P(('dp', 'mem'))
- value_grad: float32 [2048, 4096], P('mem', 'dp')
Inputs may be any that keep to these rules, and one draw needn't show every extreme that they name: `slot_pos`: each token's 32 positions are distinct. For each device and owner o, the positions used are o * 32 + j with j below a count c of 1 to 32; in each group of devices along mem, one owner has c = 32 from every device. `touched`: for each device and owner, the entries at the used positions are distinct; entries at unused positions are arbitrary rows.
All inputs are finite; a program needn't handle non-finite values.
Results may differ from a plain program's by a relative error of at most 0.001.
Values may be sent and summed in bfloat16 or wider, within the bound.
A program may use at most 256 MiB of HBM per device.

v0:
```python
import jax
import jax.numpy as jnp
from jax import lax
from jax.sharding import PartitionSpec as P


def on_device(slot_weight, slot_pos, touched, values, cotangent):
    tok_rows = slot_pos.shape[0]
    lists = touched[0]
    groups = lists.shape[0]
    cap_rows = lists.shape[1]
    spread = groups * cap_rows
    feature = cotangent.shape[1]
    owned = values.shape[0]
    dense_w = jnp.zeros((tok_rows, spread), jnp.bfloat16)
    dense_w = dense_w.at[jnp.arange(tok_rows)[:, None], slot_pos].set(slot_weight)
    partial_grad = lax.dot_general(
        dense_w, cotangent, (((0,), (0,)), ((), ())), preferred_element_type=jnp.float32
    )
    partial_grad = partial_grad.reshape(groups, cap_rows, feature)
    got_lists = lax.all_to_all(lists, "mem", split_axis=0, concat_axis=0, tiled=True)
    fetched = values[got_lists.reshape(-1)].reshape(groups, cap_rows, feature)
    arrived = lax.all_to_all(fetched, "mem", split_axis=0, concat_axis=0, tiled=True).reshape(
        spread, feature
    )
    memory_out = jnp.dot(dense_w, arrived, preferred_element_type=jnp.float32).astype(jnp.bfloat16)
    scores = lax.dot_general(
        cotangent, arrived, (((1,), (1,)), ((), ())), preferred_element_type=jnp.float32
    )
    weight_grad = jnp.take_along_axis(scores, slot_pos, axis=1)
    got_grads = lax.all_to_all(partial_grad, "mem", split_axis=0, concat_axis=0, tiled=True)
    owner_table = jax.ops.segment_sum(
        got_grads.reshape(-1, feature), got_lists.reshape(-1), num_segments=owned
    )
    value_grad = lax.psum_scatter(owner_table, "dp", scatter_dimension=1, tiled=True)
    return (memory_out, weight_grad, value_grad)


def solution(mesh):
    return jax.shard_map(
        on_device,
        mesh=mesh,
        in_specs=(
            P(("dp", "mem"), None),
            P(("dp", "mem"), None),
            P(("dp", "mem"), None, None),
            P("mem", None),
            P(("dp", "mem"), None),
        ),
        out_specs=(P(("dp", "mem"), None), P(("dp", "mem"), None), P("mem", "dp")),
        check_vma=False,
    )
```

profile of v0, /device:TPU:0, one launch (start us, length us, event | category | flops | bytes accessed | tf_op | source)
XLA Modules:
  0.0 255.3 jit_solution(10632762725211279869)
XLA Ops:
  7.2 0.0 copy-start
  7.2 7.4 %all-to-all-start = ((s32[8,1,32]{2,1,0:T(1,128)}), s32[8,1,32]{2,1,0:T(1,128)S(1)}, u32[]{:S(2)}, u32[]{:S(2)}) async-start(s32[8,1,32]{2,1,0:T(1,128)} %bitcast.26), calls=%async_computation | async-start | bytes 8192 | tf_op jit(solution)/shard_map/all_to_all | solution.py:21
  14.6 0.8 copy.26
  15.4 0.1 reshape.96
  15.5 0.8 copy.20
  16.3 0.1 copy.24
  16.4 0.8 and_reduce_fusion
  17.1 0.7 multiply_reduce_fusion
  17.9 0.1 copy.25
  18.0 0.1 reshape.94
  18.0 28.6 %scatter_custom_fusion.1 = bf16[32768]{0:T(1024)(128)(2,1)S(1)} fusion(s32[4096]{0:T(1024)S(1)} %reshape.94, bf16[4096]{0:T(1024)(128)(2,1)S(1)} %reshape.96, bf16[]{:T(256)} %constant.7.clone.1), kind=kCustom, calls=%fused_computation.13 | custom fusion | bytes 65538
  46.7 3.9 %fusion.5 = f32[256,4096]{1,0:T(8,128)} fusion(bf16[128,256]{1,0:T(8,128)(2,1)S(1)} %reshape.71, bf16[128,4096]{1,0:T(8,128)(2,1)} %param.9), kind=kOutput, calls=%fused_computation.20 | convolution fusion | flops 268435456 | bytes 5308416 | tf_op jit(solution)/shard_map/dot_general | solution.py:17
  50.6 0.0 all-to-all-done
  50.6 6.0 %all-to-all-start.2 = ((f32[8,32,4096]{2,1,0:T(8,128)}), f32[8,32,4096]{2,1,0:T(8,128)}, u32[]{:S(2)}, u32[]{:S(2)}) async-start(f32[8,32,4096]{2,1,0:T(8,128)} %bitcast.22), calls=%async_computation.2 | async-start | bytes 8388608 | tf_op jit(solution)/shard_map/all_to_all | solution.py:31
  56.6 0.0 reduce-scatter.2.cloned.1.call-start
  56.6 0.1 reshape.88
  56.7 92.6 %all-to-all-done.2 = f32[8,32,4096]{2,1,0:T(8,128)} async-done(((f32[8,32,4096]{2,1,0:T(8,128)}), f32[8,32,4096]{2,1,0:T(8,128)}, u32[]{:S(2)}, u32[]{:S(2)}) %all-to-all-start.2) | async-done | bytes 4194336 | tf_op jit(solution)/shard_map/all_to_all | solution.py:31
  149.3 9.6 %scatter_custom_fusion = f32[256,4096]{1,0:T(8,128)} fusion(s32[256]{0:T(256)S(1)} %reshape.88, f32[256,4096]{1,0:T(8,128)} %bitcast.7, f32[]{:T(128)} %constant.12.clone.1), kind=kCustom, calls=%fused_computation.5 | custom fusion | flops 1048576 | bytes 4194816 | tf_op jit(solution)/shard_map/scatter-add | solution.py:32
  159.0 0.0 reduce-scatter.2.cloned.1.call-update
  159.0 0.5 broadcast.58
  159.5 0.7 reduce.9
  160.2 0.1 reshape.63
  160.3 0.0 copy-done
  160.3 3.2 %gather_fusion = bf16[256,4096]{1,0:T(8,128)(2,1)} fusion(bf16[256,4096]{1,0:T(8,128)(2,1)S(1)} %copy-done, s32[1024]{0:T(1024)S(1)} %pad_clamp_fusion), kind=kCustom, calls=%fused_computation | custom fusion | bytes 4195328 | tf_op jit(solution)/shard_map/gather | solution.py:22
  163.5 0.0 copy-start.1
  163.5 4.5 %all-to-all-start.1 = ((bf16[8,32,4096]{2,1,0:T(8,128)(2,1)}), bf16[8,32,4096]{2,1,0:T(8,128)(2,1)}, u32[]{:S(2)}, u32[]{:S(2)}) async-start(bf16[8,32,4096]{2,1,0:T(8,128)(2,1)} %bitcast.23), calls=%async_computation.1 | async-start | bytes 4194304 | tf_op jit(solution)/shard_map/all_to_all | solution.py:23
  168.0 0.1 reshape.80
  168.1 47.7 %all-to-all-done.1 = bf16[8,32,4096]{2,1,0:T(8,128)(2,1)} async-done(((bf16[8,32,4096]{2,1,0:T(8,128)(2,1)}), bf16[8,32,4096]{2,1,0:T(8,128)(2,1)}, u32[]{:S(2)}, u32[]{:S(2)}) %all-to-all-start.1) | async-done | bytes 2097184 | tf_op jit(solution)/shard_map/all_to_all | solution.py:23
  215.8 0.0 copy-done.1
  215.8 2.3 convolution_bitcast_fusion
  218.1 26.5 %gather_fusion.1 = f32[4096]{0:T(1024)S(1)} fusion(f32[128,256]{0,1:T(8,128)S(1)} %convolution_bitcast_fusion, s32[4096]{0:T(1024)S(1)} %reshape.80), kind=kCustom, calls=%fused_computation.1 | custom fusion | bytes 65536 | tf_op jit(solution)/shard_map/jit(take_along_axis)/gather | solution.py:30
  244.6 0.1 reshape.83
  244.7 0.7 copy.27
  245.4 3.0 %convolution_convert_fusion = bf16[128,4096]{1,0:T(8,128)(2,1)} fusion(bf16[128,256]{1,0:T(8,128)(2,1)S(1)} %reshape.71, bf16[256,4096]{1,0:T(8,128)(2,1)} %bitcast.4), kind=kOutput, calls=%fused_computation.4 | convolution fusion | flops 268959744 | bytes 3211264 | tf_op jit(solution)/shard_map/dot_general | solution.py:26
  248.4 0.0 reduce-scatter.2.cloned.1.call-done
  (8 shorter events, 0.1 us)
Async XLA Ops:
  7.2 153.1 %copy-start = (bf16[256,4096]{1,0:T(8,128)(2,1)S(1)}, bf16[256,4096]{1,0:T(8,128)(2,1)}, u32[]{:S(2)}) copy-start(bf16[256,4096]{1,0:T(8,128)(2,1)} %param.8) | copy-start | bytes 6291460
  7.2 43.4 %all-to-all-start = ((s32[8,1,32]{2,1,0:T(1,128)}), s32[8,1,32]{2,1,0:T(1,128)S(1)}, u32[]{:S(2)}, u32[]{:S(2)}) async-start(s32[8,1,32]{2,1,0:T(1,128)} %bitcast.26), calls=%async_computation | async-start | bytes 8192 | tf_op jit(solution)/shard_map/all_to_all | solution.py:21
  50.6 98.7 %all-to-all-start.2 = ((f32[8,32,4096]{2,1,0:T(8,128)}), f32[8,32,4096]{2,1,0:T(8,128)}, u32[]{:S(2)}, u32[]{:S(2)}) async-start(f32[8,32,4096]{2,1,0:T(8,128)} %bitcast.22), calls=%async_computation.2 | async-start | bytes 8388608 | tf_op jit(solution)/shard_map/all_to_all | solution.py:31
  56.6 191.9 %reduce-scatter.2.cloned.1.call-start = ((), (), s32[]{:S(2)}) async-start(), calls=%async_computation.4 | async-start | bytes 5242880 | tf_op jit(solution)/shard_map/reduce_scatter | solution.py:35
  163.5 52.3 %copy-start.1 = (bf16[128,4096]{1,0:T(8,128)(2,1)S(1)}, bf16[128,4096]{1,0:T(8,128)(2,1)}, u32[]{:S(2)}) copy-start(bf16[128,4096]{1,0:T(8,128)(2,1)} %param.9) | copy-start | bytes 3145732
  163.5 52.3 %all-to-all-start.1 = ((bf16[8,32,4096]{2,1,0:T(8,128)(2,1)}), bf16[8,32,4096]{2,1,0:T(8,128)(2,1)}, u32[]{:S(2)}, u32[]{:S(2)}) async-start(bf16[8,32,4096]{2,1,0:T(8,128)(2,1)} %bitcast.23), calls=%async_computation.1 | async-start | bytes 4194304 | tf_op jit(solution)/shard_map/all_to_all | solution.py:23
Sparse Core Ops, SparseCore 0:
  159.1 43.5 reduce-scatter.1
where the time goes:
time: 256 us; the launch traced here: 255 us
  waiting for transfers between devices  140 us (55%)
  local copies, waits for them, and re-layouts  61.8 us (24%)
  starting transfers between devices  17.9 us (7%)
  between operations  14.1 us (6%)
  other arithmetic  11.9 us (5%)
  matrix products  9.2 us (4%)
    all_to_all x1, waiting for transfers between devices, on_device(): lax.all_to_all(partial_grad, 'mem', split_axis=0, concat_axis=0, tiled=True)  92.6 us
    all_to_all x1, waiting for transfers between devices, on_device(): lax.all_to_all(fetched, 'mem', split_axis=0, concat_axis=0, tiled=True)  47.7 us
    unnamed x11, local copies, waits for them, and re-layouts  31.2 us
    gather x2, local copies, waits for them, and re-layouts, on_device(): weight_grad = jnp.take_along_axis(scores, slot_pos, axis=1)  26.6 us
    scatter-add x1, other arithmetic, on_device(): jax.ops.segment_sum(got_grads.reshape(-1, feature), got_lists.reshape(-1)...  9.65 us
    all_to_all x1, starting transfers between devices, on_device(): lax.all_to_all(lists, 'mem', split_axis=0, concat_axis=0, tiled=True)  7.4 us
    all_to_all x1, starting transfers between devices, on_device(): lax.all_to_all(partial_grad, 'mem', split_axis=0, concat_axis=0, tiled=True)  5.99 us
  transfers between devices with their start and end apart: 4, of which 2 were waited for; matrix products, arithmetic and copies ran while one was open for 29% of the time, Pallas kernels for 0%

commit v1 on v0

v1 whole, which is shorter than its diff:
```python
import functools

import jax
import jax.numpy as jnp
from jax import lax
from jax.experimental import pallas as pl
from jax.experimental.pallas import tpu as pltpu
from jax.sharding import PartitionSpec as P

MESH = pl.DeviceIdType.MESH
STEPS = 32000.0


def iota(shape, axis):
    return lax.broadcasted_iota(jnp.int32, shape, axis)


def coded(x):
    top = jnp.max(jnp.abs(x), axis=1, keepdims=True)
    step = jnp.maximum(top * (1.0 / STEPS), 1e-30).astype(jnp.bfloat16).astype(jnp.float32)
    return jnp.round(x * (1.0 / step)).astype(jnp.int32).astype(jnp.int16), step


def pieces(q):
    full = q.astype(jnp.int32).astype(jnp.float32)
    high = full.astype(jnp.bfloat16)
    return high, (full - high.astype(jnp.float32)).astype(jnp.bfloat16)


def decoded_sum(hot, q):
    high, low = pieces(q)
    return jnp.dot(hot, high, preferred_element_type=jnp.float32) + jnp.dot(
        hot, low, preferred_element_type=jnp.float32
    )


def kernel(
    n_dp, n_mem,
    lists_ref, pos_ref, w_ref, cot_ref, values_ref,
    out_ref, wgrad_ref, vgrad_ref,
    dense_w, step_mine, step_got, lists_got, coded_mine, coded_got, hot, vals, picked, arrived,
    sum_mine, sum_coded, sum_got, sum_step, sum_step_got,
    list_ss, list_rs, step_ss, step_rs, grad_ss, grad_rs, val_ss, val_rs, pair_ss, pair_rs, own_sem,
):
    half = n_mem // 2
    group = n_dp * half
    cap = lists_ref.shape[1]
    toks, topk = pos_ref.shape
    rows = values_ref.shape[0]
    cols = cot_ref.shape[1] // n_dp
    spread = n_mem * cap
    bits = cap.bit_length() - 1
    dp = lax.axis_index("dp")
    mem = lax.axis_index("mem")
    here = lax.rem(mem, half)
    base = mem - here
    mirror = lax.rem(mem + half, n_mem)
    other_base = half - base
    me = dp * half + here

    def place(t):
        d = lax.rem(dp + 1 + t // half, n_dp)
        h = lax.rem(here + 1 + lax.rem(t, half), half)
        return d, h, d * half + h

    def every(fn, first=0, last=group - 1):
        def body(t, c):
            fn(*place(t))
            return c
        lax.fori_loop(first, last, body, 0)

    def remote(src, dst, ss, rs, d, m):
        return pltpu.make_async_remote_copy(
            src_ref=src, dst_ref=dst, send_sem=ss, recv_sem=rs, device_id=(d, m), device_id_type=MESH
        )

    barrier = pltpu.get_barrier_semaphore()
    every(lambda d, h, g: pl.semaphore_signal(barrier, inc=1, device_id=(d, base + h), device_id_type=MESH))
    pl.semaphore_signal(barrier, inc=1, device_id=(dp, mirror), device_id_type=MESH)

    my_cols = pl.ds(pl.multiple_of(dp * cols, cols), cols)
    own = pltpu.make_async_copy(values_ref.at[:, my_cols], vals.at[0], own_sem)
    own.start()
    lists_got[me] = lists_ref[...]

    lane = iota((toks, spread), 1)
    acc = jnp.zeros((toks, spread), jnp.float32)
    for k in range(topk):
        acc = jnp.where(pos_ref[:, k : k + 1] == lane, w_ref[:, k : k + 1].astype(jnp.float32), acc)
    dense_w[...] = acc.astype(jnp.bfloat16)

    pl.semaphore_wait(barrier, group)

    def list_copy(d, h, g):
        return remote(lists_ref, lists_got.at[me], list_ss.at[g], list_rs.at[me], d, base + h)

    every(lambda d, h, g: list_copy(d, h, g).start())
    pair_vals = remote(values_ref.at[:, my_cols], vals.at[1], pair_ss.at[0], pair_rs.at[0], dp, mirror)
    pair_vals.start()

    def grad_copy(o, d, h, g):
        m = (other_base if o else base) + h
        return remote(
            coded_mine.at[d, m], coded_got.at[o, me], grad_ss.at[o, g], grad_rs.at[o, me], d, base + h
        )

    def step_copy(d, h, g):
        return remote(step_mine.at[d], step_got.at[me], step_ss.at[g], step_rs.at[me], d, base + h)

    to_owner = (iota((n_mem, spread), 1) >> bits == iota((n_mem, spread), 0)).astype(jnp.bfloat16)
    to_lane = iota((spread, cap), 0) & (cap - 1) == iota((spread, cap), 1)
    for i in range(n_dp):
        d_now = lax.rem(dp + 1 + i, n_dp)
        block = cot_ref[:, pl.ds(pl.multiple_of(d_now * cols, cols), cols)]
        terms = lax.dot_general(
            dense_w[...], block, (((0,), (0,)), ((), ())), preferred_element_type=jnp.float32
        )
        q, step = coded(terms)
        coded_mine[d_now] = q.reshape(n_mem, cap, cols)
        step_mine[d_now] = jnp.dot(
            to_owner, jnp.where(to_lane, step, 0.0).astype(jnp.bfloat16), preferred_element_type=jnp.float32
        )
        first, last = i * half, min((i + 1) * half, group - 1)
        every(lambda d, h, g: step_copy(d, h, g).start(), first, last)
        every(lambda d, h, g: grad_copy(1, d, h, g).start(), first, last)
        every(lambda d, h, g: grad_copy(0, d, h, g).start(), first, last)
    step_got[me] = step_mine[dp]
    coded_got[0, me] = coded_mine[dp, mem]
    coded_got[1, me] = coded_mine[dp, mirror]

    every(lambda d, h, g: remote(lists_ref, lists_got.at[g], list_ss.at[g], list_rs.at[g], d, base + h).wait_recv())
    slots = group * cap
    fan = (iota((cap, slots), 1) & (cap - 1) == iota((cap, slots), 0)).astype(jnp.bfloat16)
    diag = iota((group, slots), 1) >> bits == iota((group, slots), 0)

    def along_lanes(table, m):
        pick = iota(table.shape, 1) == m
        part = jnp.sum(jnp.where(pick, table, 0.0), axis=1).astype(jnp.bfloat16)
        wide = jnp.dot(part, fan, preferred_element_type=jnp.float32)
        return jnp.sum(jnp.where(diag, wide, 0.0), axis=0, keepdims=True)

    lists_f = lists_got[...].astype(jnp.float32)
    row_of = iota((rows, slots), 0).astype(jnp.float32)

    def val_copy(o, d, h, g):
        m = mirror if o else mem
        return remote(
            picked.at[o, g], arrived.at[m, :, my_cols], val_ss.at[o, g], val_rs.at[o, me], d, base + h
        )

    some = min(group, 16)

    def select(o):
        def body(b, c):
            lanes = pl.ds(pl.multiple_of(b * some * cap, some * cap), some * cap)
            got = lax.dot_general(
                hot[o, :, lanes], vals[o], (((0,), (0,)), ((), ())), preferred_element_type=jnp.float32
            )
            picked[o, pl.ds(b * some, some)] = got.astype(jnp.bfloat16).reshape(some, cap, cols)
            return c
        lax.fori_loop(0, group // some, body, 0)

    for o, m in ((0, mem), (1, mirror)):
        hot[o] = (row_of == along_lanes(lists_f, m)).astype(jnp.bfloat16)
    own.wait()
    select(0)
    every(lambda d, h, g: val_copy(0, d, h, g).start())
    arrived[mem, :, my_cols] = picked[0, me]
    pair_vals.wait_recv()
    select(1)
    every(lambda d, h, g: val_copy(1, d, h, g).start())
    arrived[mirror, :, my_cols] = picked[1, me]

    every(lambda d, h, g: remote(step_mine.at[0], step_got.at[g], step_ss.at[g], step_rs.at[g], d, base + h).wait_recv())
    steps = step_got[...]

    def gathered(o, m):
        every(
            lambda d, h, g: remote(
                coded_mine.at[0, 0], coded_got.at[o, g], grad_ss.at[o, g], grad_rs.at[o, g], d, base + h
            ).wait_recv()
        )
        scaled = (hot[o].astype(jnp.float32) * along_lanes(steps, m)).astype(jnp.bfloat16)
        return decoded_sum(scaled, coded_got[o].reshape(slots, cols))

    q, step = coded(gathered(1, mirror))
    sum_coded[...] = q
    eye = iota((rows, rows), 0) == iota((rows, rows), 1)
    sum_step[...] = jnp.broadcast_to(jnp.sum(jnp.where(eye, step, 0.0), axis=0, keepdims=True), sum_step.shape)
    pair_step = remote(sum_step, sum_step_got, pair_ss.at[1], pair_rs.at[1], dp, mirror)
    pair_step.start()
    pair_sum = remote(sum_coded, sum_got, pair_ss.at[2], pair_rs.at[2], dp, mirror)
    pair_sum.start()
    sum_mine[...] = gathered(0, mem)

    def val_wait(o, d, h, g):
        m = (other_base if o else base) + h
        cols_d = pl.ds(pl.multiple_of(d * cols, cols), cols)
        remote(
            picked.at[o, g], arrived.at[m, :, cols_d], val_ss.at[o, g], val_rs.at[o, g], d, base + h
        ).wait_recv()

    every(lambda d, h, g: val_wait(0, d, h, g))
    every(lambda d, h, g: val_wait(1, d, h, g))

    def tokens(b, scores):
        at = pl.ds(pl.multiple_of(b * cols, cols), cols)
        table = arrived[:, :, at].reshape(spread, cols)
        out_ref[:, at] = jnp.dot(dense_w[...], table, preferred_element_type=jnp.float32).astype(out_ref.dtype)
        return scores + lax.dot_general(
            cot_ref[:, at], table, (((1,), (1,)), ((), ())), preferred_element_type=jnp.float32
        )

    scores = lax.fori_loop(0, n_dp, tokens, jnp.zeros((toks, spread), jnp.float32))
    slot = iota((toks, topk), 1)
    wgrad = jnp.zeros((toks, topk), jnp.float32)
    for k in range(topk):
        one = jnp.sum(jnp.where(pos_ref[:, k : k + 1] == lane, scores, 0.0), axis=1, keepdims=True)
        wgrad = jnp.where(slot == k, one, wgrad)
    wgrad_ref[...] = wgrad

    pair_step.wait_recv()
    pair_sum.wait_recv()
    scaled = jnp.where(eye, sum_step_got[0:1, :], 0.0).astype(jnp.bfloat16)
    vgrad_ref[...] = sum_mine[...] + decoded_sum(scaled, sum_got[...])

    every(lambda d, h, g: list_copy(d, h, g).wait_send())
    every(lambda d, h, g: step_copy(d, h, g).wait_send())
    for o in range(2):
        every(lambda d, h, g: grad_copy(o, d, h, g).wait_send())
        every(lambda d, h, g: val_copy(o, d, h, g).wait_send())
    pair_vals.wait_send()
    pair_step.wait_send()
    pair_sum.wait_send()


def on_device(n_dp, n_mem, slot_weight, slot_pos, touched, values, cotangent):
    toks, topk = slot_pos.shape
    lists = touched[0]
    cap = lists.shape[1]
    rows, width = values.shape
    cols = width // n_dp
    group = n_dp * n_mem // 2
    f32, bf16, i16 = jnp.float32, jnp.bfloat16, jnp.int16
    dma = pltpu.SemaphoreType.DMA
    vmem = pl.BlockSpec(memory_space=pltpu.VMEM)
    return pl.pallas_call(
        functools.partial(kernel, n_dp, n_mem),
        out_shape=(
            jax.ShapeDtypeStruct((toks, width), bf16),
            jax.ShapeDtypeStruct((toks, topk), f32),
            jax.ShapeDtypeStruct((rows, cols), f32),
        ),
        in_specs=[vmem, vmem, vmem, vmem, pl.BlockSpec(memory_space=pl.ANY)],
        out_specs=(vmem, vmem, vmem),
        scratch_shapes=[
            pltpu.VMEM((toks, n_mem * cap), bf16),
            pltpu.VMEM((n_dp, n_mem, cap), f32),
            pltpu.VMEM((group, n_mem, cap), f32),
            pltpu.VMEM((group, n_mem, cap), jnp.int32),
            pltpu.VMEM((n_dp, n_mem, cap, cols), i16),
            pltpu.VMEM((2, group, cap, cols), i16),
            pltpu.VMEM((2, rows, group * cap), bf16),
            pltpu.VMEM((2, rows, cols), bf16),
            pltpu.VMEM((2, group, cap, cols), bf16),
            pltpu.VMEM((n_mem, cap, width), bf16),
            pltpu.VMEM((rows, cols), f32),
            pltpu.VMEM((rows, cols), i16),
            pltpu.VMEM((rows, cols), i16),
            pltpu.VMEM((8, rows), f32),
            pltpu.VMEM((8, rows), f32),
            dma((group,)), dma((group,)),
            dma((group,)), dma((group,)),
            dma((2, group)), dma((2, group)),
            dma((2, group)), dma((2, group)),
            dma((3,)), dma((3,)),
            dma,
        ],
        compiler_params=pltpu.CompilerParams(
            collective_id=0, has_side_effects=True, vmem_limit_bytes=60 * 2**20
        ),
    )(lists, slot_pos, slot_weight, cotangent, values)


def solution(mesh):
    return jax.shard_map(
        functools.partial(on_device, mesh.shape["dp"], mesh.shape["mem"]),
        mesh=mesh,
        in_specs=(
            P(("dp", "mem"), None),
            P(("dp", "mem"), None),
            P(("dp", "mem"), None, None),
            P("mem", None),
            P(("dp", "mem"), None),
        ),
        out_specs=(P(("dp", "mem"), None), P(("dp", "mem"), None), P("mem", "dp")),
        check_vma=False,
    )
```

time: 256 us -> 95.6 us (0.37)
  waiting for transfers between devices: 140 us -> 0 us
  Pallas kernels: 0 us -> 86.9 us
  local copies, waits for them, and re-layouts: 61.8 us -> 7.73 us
  starting transfers between devices: 17.9 us -> 0 us
  between operations: 14.1 us -> 0.65 us
  other arithmetic: 11.9 us -> 0 us
  matrix products: 9.2 us -> 0 us
    all_to_all x3 -> x0, waiting for transfers between devices: 140 us -> none  [the longest x1 92.6 us: on_device(): lax.all_to_all(partial_grad, 'mem', split_axis=0, concat_axis=0, tiled=True)]
    pallas_call x0 -> x1, Pallas kernels: none -> 86.9 us  [on_device(): pl.pallas_call(functools.partial(kernel, n_dp, n_mem), out_shape=(jax.Sha...]
    gather x3 -> x0, local copies, waits for them, and re-layouts: 29.8 us -> none  [the longest x2 26.6 us: on_device(): weight_grad = jnp.take_along_axis(scores, slot_pos, axis=1)]
    unnamed x11 -> x6, local copies, waits for them, and re-layouts: 31.2 us -> 6.12 us
    all_to_all x3 -> x0, starting transfers between devices: 17.9 us -> none  [the longest x1 7.4 us: on_device(): lax.all_to_all(lists, 'mem', split_axis=0, concat_axis=0, tiled=True)]
    scatter-add x1 -> x0, other arithmetic: 9.65 us -> none  [on_device(): jax.ops.segment_sum(got_grads.reshape(-1, feature), got_lists.reshape(-1)...]
    dot_general x3 -> x0, matrix products: 9.2 us -> none  [the longest x1 3.88 us: on_device(): lax.dot_general(dense_w, cotangent, (((0,), (0,)), ((), ())), preferred_e...]
  transfers between devices with their start and end apart: 4 -> 0, of which waited for: 2 -> 0; matrix products, arithmetic and copies ran while one was open for 29% -> 0% of each run, Pallas kernels for 0% -> 0%
where the time goes in v1:
time: 95.6 us; the launch traced here: 95.3 us
  Pallas kernels  86.9 us (91%)
  local copies, waits for them, and re-layouts  7.73 us (8%)
    pallas_call x1, Pallas kernels, on_device(): pl.pallas_call(functools.partial(kernel, n_dp, n_mem), out_shape=(jax.Sha...  86.9 us
    unnamed x6, local copies, waits for them, and re-layouts  6.12 us

profile of v1, /device:TPU:0, one launch (start us, length us, event | category | flops | bytes accessed | tf_op | source)
XLA Modules:
  0.0 95.3 jit_solution(16601765676420078902)
XLA Ops:
  0.6 1.4 %copy.9.w_ref = bf16[128,32]{1,0:T(8,128)(2,1)} copy(bf16[128,32]{0,1:T(8,128)(2,1)} %param.5) | data formatting | bytes 16384 | tf_op args[0]
  2.0 1.4 %copy.8.pos_ref = s32[128,32]{1,0:T(8,128)} copy(s32[128,32]{0,1:T(8,128)} %param.6) | data formatting | bytes 32768 | tf_op args[1]
  3.5 86.9 %shard_map.76 = (bf16[128,4096]{1,0:T(8,128)(2,1)}, f32[128,32]{1,0:T(8,128)}, f32[256,1024]{1,0:T(8,128)}) custom-call(s32[8,32]{1,0:T(8,128)} %bitcast.1, s32[128,32]{1,0:T(8,128)} %copy.8.pos_ref, bf16[128,32]{1,0:T(8,128)(2,1)} %copy.9.w_ref, bf16[128,4096]{1,0:T(8,128)(2,1)} %cot_ref.1, bf16[256,4096]{1,0:T(8,128)(2,1)} %values_ref.1), custom_call_target="tpu_custom_call" | custom-call | tf_op jit(solution)/shard_map/pallas_call | solution.py:247
  90.4 0.0 copy-start
  90.4 1.6 %copy.10 = f32[128,32]{0,1:T(8,128)} copy(f32[128,32]{1,0:T(8,128)} %get-tuple-element.4) | data formatting | bytes 32768 | tf_op jit(solution)/shard_map/pallas_call | solution.py:247
  92.0 2.3 %copy.13 = bf16[128,4096]{1,0:T(8,128)(2,1)} copy(bf16[128,4096]{1,0:T(8,128)(2,1)} %get-tuple-element.9) | data formatting | bytes 2097152
  94.3 0.0 copy-done
  94.3 1.0 %copy.14 = f32[256,1024]{1,0:T(8,128)} copy(f32[256,1024]{1,0:T(8,128)S(1)} %copy-done) | data formatting | bytes 2097152
Async XLA Ops:
  90.4 3.9 %copy-start = (f32[256,1024]{1,0:T(8,128)S(1)}, f32[256,1024]{1,0:T(8,128)}, u32[]{:S(2)}) copy-start(f32[256,1024]{1,0:T(8,128)} %get-tuple-element.11) | copy-start | bytes 3145732

commit v2 on v1

v2 whole, which is shorter than its diff:
```python
import functools

import jax
import jax.numpy as jnp
from jax import lax
from jax.experimental import pallas as pl
from jax.experimental.pallas import tpu as pltpu
from jax.sharding import PartitionSpec as P

MESH = pl.DeviceIdType.MESH
STEPS = 32000.0


def iota(shape, axis):
    return lax.broadcasted_iota(jnp.int32, shape, axis)


def coded(x):
    top = jnp.max(jnp.abs(x), axis=1, keepdims=True)
    step = jnp.maximum(top * (1.0 / STEPS), 1e-30).astype(jnp.bfloat16).astype(jnp.float32)
    return jnp.round(x * (1.0 / step)).astype(jnp.int32).astype(jnp.int16), step


def pieces(q):
    full = q.astype(jnp.int32).astype(jnp.float32)
    high = full.astype(jnp.bfloat16)
    return high, (full - high.astype(jnp.float32)).astype(jnp.bfloat16)


def decoded_sum(hot, q):
    high, low = pieces(q)
    return jnp.dot(hot, high, preferred_element_type=jnp.float32) + jnp.dot(
        hot, low, preferred_element_type=jnp.float32
    )


def kernel(
    n_dp, n_mem, n_x,
    lists_ref, pos_ref, w_ref, cot_ref, values_ref,
    out_ref, wgrad_ref, vgrad_ref,
    dense_w, step_mine, step_got, lists_got, coded_mine, coded_got, hot, vals, picked, arrived,
    sum_mine, sum_coded, sum_got, sum_step, sum_step_got,
    list_ss, list_rs, step_ss, step_rs, grad_ss, grad_rs, val_ss, val_rs,
    line_ss, line_rs, sum_ss, sum_rs, own_sem,
):
    n_z = n_mem // n_x
    group = n_dp * n_x
    cap = lists_ref.shape[1]
    topk, toks = pos_ref.shape
    rows = values_ref.shape[0]
    cols = cot_ref.shape[1] // n_dp
    spread = n_mem * cap
    bits = cap.bit_length() - 1
    dp = lax.axis_index("dp")
    mem = lax.axis_index("mem")
    z = mem // n_x
    x = lax.rem(mem, n_x)
    me = dp * n_x + x
    has_below, has_above = z > 0, z < n_z - 1

    def place(t):
        d = lax.rem(dp + 1 + t // n_x, n_dp)
        h = lax.rem(x + 1 + lax.rem(t, n_x), n_x)
        return d, h, d * n_x + h

    def every(fn):
        def body(t, c):
            fn(*place(t))
            return c
        lax.fori_loop(0, group - 1, body, 0)

    def remote(src, dst, ss, rs, d, m):
        return pltpu.make_async_remote_copy(
            src_ref=src, dst_ref=dst, send_sem=ss, recv_sem=rs, device_id=(d, m), device_id_type=MESH
        )

    def plane(src, dst, ss, rs, d, h):
        return remote(src, dst, ss, rs, d, z * n_x + h)

    barrier = pltpu.get_barrier_semaphore()

    def greet(m):
        pl.semaphore_signal(barrier, inc=1, device_id=(dp, m), device_id_type=MESH)

    every(
        lambda d, h, g: pl.semaphore_signal(
            barrier, inc=1, device_id=(d, z * n_x + h), device_id_type=MESH
        )
    )
    pl.when(has_below)(lambda: greet(mem - n_x))
    pl.when(has_above)(lambda: greet(mem + n_x))

    my_cols = pl.ds(pl.multiple_of(dp * cols, cols), cols)
    own = pltpu.make_async_copy(values_ref.at[:, my_cols], vals.at[z], own_sem)
    own.start()
    lists_got[me] = lists_ref[...]

    place_of = iota((spread, toks), 0)
    acc = jnp.zeros((spread, toks), jnp.float32)
    weights = w_ref[...].astype(jnp.float32)
    for k in range(topk):
        acc = jnp.where(pos_ref[k : k + 1, :] == place_of, weights[k : k + 1, :], acc)
    dense_w[...] = acc.astype(jnp.bfloat16)

    pl.semaphore_wait(barrier, group - 1 + has_below.astype(jnp.int32) + has_above.astype(jnp.int32))

    def line_copy(k, up):
        way = 1 if up else 0
        return remote(
            vals.at[k], vals.at[k], line_ss.at[way, k], line_rs.at[k], dp, mem + n_x if up else mem - n_x
        )

    def pass_on(k, up):
        pl.when(has_above if up else has_below)(lambda: line_copy(k, up).start())

    def list_copy(d, h, g):
        return plane(lists_ref, lists_got.at[me], list_ss.at[g], list_rs.at[me], d, h)

    every(lambda d, h, g: list_copy(d, h, g).start())
    own.wait()
    pass_on(z, True)
    pass_on(z, False)

    def grad_copy(k, d, h, g):
        return plane(
            coded_mine.at[d, k * n_x + h], coded_got.at[k, me], grad_ss.at[k, g], grad_rs.at[k, me], d, h
        )

    def step_copy(d, h, g):
        return plane(step_mine.at[d], step_got.at[me], step_ss.at[g], step_rs.at[me], d, h)

    to_owner = (iota((n_mem, spread), 1) >> bits == iota((n_mem, spread), 0)).astype(jnp.bfloat16)
    to_lane = iota((spread, cap), 0) & (cap - 1) == iota((spread, cap), 1)

    def terms_of(d, c):
        block = cot_ref[:, pl.ds(pl.multiple_of(d * cols, cols), cols)]
        q, step = coded(jnp.dot(dense_w[...], block, preferred_element_type=jnp.float32))
        coded_mine[d] = q.reshape(n_mem, cap, cols)
        step_mine[d] = jnp.dot(
            to_owner, jnp.where(to_lane, step, 0.0).astype(jnp.bfloat16), preferred_element_type=jnp.float32
        )
        return c

    lax.fori_loop(0, n_dp, terms_of, 0)
    every(lambda d, h, g: step_copy(d, h, g).start())
    outer_first = [k for pair in zip(range(n_z), reversed(range(n_z))) for k in pair][:n_z]
    for k in outer_first:
        every(lambda d, h, g: grad_copy(k, d, h, g).start())
        coded_got[k, me] = coded_mine[dp, k * n_x + x]
    step_got[me] = step_mine[dp]

    every(lambda d, h, g: plane(lists_ref, lists_got.at[g], list_ss.at[g], list_rs.at[g], d, h).wait_recv())
    slots = group * cap
    fan = (iota((cap, slots), 1) & (cap - 1) == iota((cap, slots), 0)).astype(jnp.bfloat16)
    diag = iota((group, slots), 1) >> bits == iota((group, slots), 0)

    def along_lanes(table, m):
        pick = iota(table.shape, 1) == m
        part = jnp.sum(jnp.where(pick, table, 0.0), axis=1).astype(jnp.bfloat16)
        wide = jnp.dot(part, fan, preferred_element_type=jnp.float32)
        return jnp.sum(jnp.where(diag, wide, 0.0), axis=0, keepdims=True)

    row_of = iota((rows, slots), 0).astype(jnp.float32)

    def hot_of(k, c):
        lists_f = lists_got[...].astype(jnp.float32)
        hot[k] = (row_of == along_lanes(lists_f, k * n_x + x)).astype(jnp.bfloat16)
        return c

    lax.fori_loop(0, n_z, hot_of, 0)

    def val_copy(k, d, h, g):
        return plane(
            picked.at[k, g], arrived.at[k * n_x + x, :, my_cols], val_ss.at[k, g], val_rs.at[k, me], d, h
        )

    def select(k):
        got = lax.dot_general(
            hot[k], vals[k], (((0,), (0,)), ((), ())), preferred_element_type=jnp.float32
        )
        picked[k] = got.astype(jnp.bfloat16).reshape(group, cap, cols)
        every(lambda d, h, g: val_copy(k, d, h, g).start())
        arrived[k * n_x + x, :, my_cols] = picked[k, me]

    select(z)

    every(
        lambda d, h, g: plane(step_mine.at[0], step_got.at[g], step_ss.at[g], step_rs.at[g], d, h).wait_recv()
    )
    eye = iota((rows, rows), 0) == iota((rows, rows), 1)

    def gathered(k):
        every(
            lambda d, h, g: plane(
                coded_mine.at[0, 0], coded_got.at[k, g], grad_ss.at[k, g], grad_rs.at[k, g], d, h
            ).wait_recv()
        )
        scaled = (hot[k].astype(jnp.float32) * along_lanes(step_got[...], k * n_x + x)).astype(jnp.bfloat16)
        return decoded_sum(scaled, coded_got[k].reshape(slots, cols))

    def sum_copies(k, up):
        to = mem + n_x if up else mem - n_x
        at = jnp.where(k == z + 1, n_z, k) if up else k
        return (
            remote(sum_step.at[k], sum_step_got.at[at], sum_ss.at[0, k], sum_rs.at[0, at], dp, to),
            remote(sum_coded.at[k], sum_got.at[at], sum_ss.at[1, k], sum_rs.at[1, at], dp, to),
        )

    def received(at):
        remote(sum_step.at[0], sum_step_got.at[at], sum_ss.at[0, 0], sum_rs.at[0, at], dp, mem).wait_recv()
        remote(sum_coded.at[0], sum_got.at[at], sum_ss.at[1, 0], sum_rs.at[1, at], dp, mem).wait_recv()
        scaled = jnp.where(eye, sum_step_got[at][0:1, :], 0.0).astype(jnp.bfloat16)
        return decoded_sum(scaled, sum_got[at])

    def relay(k, up, first):
        sum_mine[...] = gathered(k)

        @pl.when(jnp.logical_not(first))
        def _():
            sum_mine[...] += received(k)

        q, step = coded(sum_mine[...])
        sum_coded[k] = q
        sum_step[k] = jnp.broadcast_to(
            jnp.sum(jnp.where(eye, step, 0.0), axis=0, keepdims=True), sum_step.shape[1:]
        )
        for copy in sum_copies(k, up):
            copy.start()

    def take(k, up):
        line_copy(k, up).wait_recv()
        pass_on(k, up)
        select(k)

    def step_along(s, c):
        @pl.when(s > 0)
        def _():
            pl.when(z - s >= 0)(lambda: take(z - s, True))
            pl.when(z + s < n_z)(lambda: take(z + s, False))

        down = s - (n_z - 1 - z)
        pl.when((down >= 0) & (down < z))(lambda: relay(down, False, z == n_z - 1))
        up = n_z - 1 - s + z
        pl.when((up > z) & (up < n_z))(lambda: relay(up, True, z == 0))
        return c

    lax.fori_loop(0, n_z, step_along, 0)
    sum_mine[...] = gathered(z)

    def val_wait(k, d, h, g):
        cols_d = pl.ds(pl.multiple_of(d * cols, cols), cols)
        plane(
            picked.at[k, g], arrived.at[k * n_x + h, :, cols_d], val_ss.at[k, g], val_rs.at[k, g], d, h
        ).wait_recv()

    for k in range(n_z):
        every(lambda d, h, g: val_wait(k, d, h, g))

    def tokens(b, scores):
        at = pl.ds(pl.multiple_of(b * cols, cols), cols)
        table = arrived[:, :, at].reshape(spread, cols)
        out_ref[:, at] = lax.dot_general(
            dense_w[...], table, (((0,), (0,)), ((), ())), preferred_element_type=jnp.float32
        ).astype(out_ref.dtype)
        return scores + lax.dot_general(
            table, cot_ref[:, at], (((1,), (1,)), ((), ())), preferred_element_type=jnp.float32
        )

    scores = lax.fori_loop(0, n_dp, tokens, jnp.zeros((spread, toks), jnp.float32))
    for k in range(topk):
        wgrad_ref[k : k + 1, :] = jnp.sum(
            jnp.where(pos_ref[k : k + 1, :] == place_of, scores, 0.0), axis=0, keepdims=True
        )

    @pl.when(has_above)
    def _():
        sum_mine[...] += received(z)

    @pl.when(has_below)
    def _():
        sum_mine[...] += received(n_z)

    vgrad_ref[...] = sum_mine[...]

    every(lambda d, h, g: list_copy(d, h, g).wait_send())
    every(lambda d, h, g: step_copy(d, h, g).wait_send())

    def sent(k, c):
        every(lambda d, h, g: grad_copy(k, d, h, g).wait_send())
        every(lambda d, h, g: val_copy(k, d, h, g).wait_send())
        for up in (False, True):
            pl.when((has_above & (k <= z)) if up else (has_below & (k >= z)))(
                lambda: line_copy(k, up).wait_send()
            )

            @pl.when((k > z) if up else (k < z))
            def _():
                for copy in sum_copies(k, up):
                    copy.wait_send()
        return c

    lax.fori_loop(0, n_z, sent, 0)


def on_device(n_dp, n_mem, slot_weight, slot_pos, touched, values, cotangent):
    toks, topk = slot_pos.shape
    lists = touched[0]
    cap = lists.shape[1]
    rows, width = values.shape
    cols = width // n_dp
    n_x = 1
    while 4 * n_x * n_x <= n_mem:
        n_x *= 2
    n_z = n_mem // n_x
    group = n_dp * n_x
    f32, bf16, i16 = jnp.float32, jnp.bfloat16, jnp.int16
    dma = pltpu.SemaphoreType.DMA
    vmem = pl.BlockSpec(memory_space=pltpu.VMEM)
    out, wgrad, vgrad = pl.pallas_call(
        functools.partial(kernel, n_dp, n_mem, n_x),
        out_shape=(
            jax.ShapeDtypeStruct((toks, width), bf16),
            jax.ShapeDtypeStruct((topk, toks), f32),
            jax.ShapeDtypeStruct((rows, cols), f32),
        ),
        in_specs=[vmem, vmem, vmem, vmem, pl.BlockSpec(memory_space=pl.ANY)],
        out_specs=(vmem, vmem, vmem),
        scratch_shapes=[
            pltpu.VMEM((n_mem * cap, toks), bf16),
            pltpu.VMEM((n_dp, n_mem, cap), f32),
            pltpu.VMEM((group, n_mem, cap), f32),
            pltpu.VMEM((group, n_mem, cap), jnp.int32),
            pltpu.VMEM((n_dp, n_mem, cap, cols), i16),
            pltpu.VMEM((n_z, group, cap, cols), i16),
            pltpu.VMEM((n_z, rows, group * cap), bf16),
            pltpu.VMEM((n_z, rows, cols), bf16),
            pltpu.VMEM((n_z, group, cap, cols), bf16),
            pltpu.VMEM((n_mem, cap, width), bf16),
            pltpu.VMEM((rows, cols), f32),
            pltpu.VMEM((n_z, rows, cols), i16),
            pltpu.VMEM((n_z + 1, rows, cols), i16),
            pltpu.VMEM((n_z, 8, rows), f32),
            pltpu.VMEM((n_z + 1, 8, rows), f32),
            dma((group,)), dma((group,)),
            dma((group,)), dma((group,)),
            dma((n_z, group)), dma((n_z, group)),
            dma((n_z, group)), dma((n_z, group)),
            dma((2, n_z)), dma((n_z,)),
            dma((2, n_z)), dma((2, n_z + 1)),
            dma,
        ],
        compiler_params=pltpu.CompilerParams(
            collective_id=0, has_side_effects=True, vmem_limit_bytes=60 * 2**20
        ),
    )(lists, slot_pos.T, slot_weight.T, cotangent, values)
    return out, wgrad.T, vgrad


def solution(mesh):
    return jax.shard_map(
        functools.partial(on_device, mesh.shape["dp"], mesh.shape["mem"]),
        mesh=mesh,
        in_specs=(
            P(("dp", "mem"), None),
            P(("dp", "mem"), None),
            P(("dp", "mem"), None, None),
            P("mem", None),
            P(("dp", "mem"), None),
        ),
        out_specs=(P(("dp", "mem"), None), P(("dp", "mem"), None), P("mem", "dp")),
        check_vma=False,
    )
```

time: 95.6 us -> 70.9 us (0.74)
  Pallas kernels: 86.9 us -> 66.1 us
  local copies, waits for them, and re-layouts: 7.73 us -> 3.96 us
    pallas_call x1, Pallas kernels: 86.9 us -> 66.1 us  [on_device(): pl.pallas_call(functools.partial(kernel, n_dp, n_mem, n_x), out_shape=(ja...]
    unnamed x6 -> x7, local copies, waits for them, and re-layouts: 6.12 us -> 3.96 us
    pallas_call x1 -> x0, local copies, waits for them, and re-layouts: 1.61 us -> none  [on_device(): pl.pallas_call(functools.partial(kernel, n_dp, n_mem), out_shape=(jax.Sha...]
where the time goes in v2:
time: 70.9 us; the launch traced here: 70.7 us
  Pallas kernels  66.1 us (93%)
  local copies, waits for them, and re-layouts  3.96 us (6%)
    pallas_call x1, Pallas kernels, on_device(): pl.pallas_call(functools.partial(kernel, n_dp, n_mem, n_x), out_shape=(ja...  66.1 us
    unnamed x7, local copies, waits for them, and re-layouts  3.96 us

profile of v2, /device:TPU:0, one launch (start us, length us, event | category | flops | bytes accessed | tf_op | source)
XLA Modules:
  0.0 70.7 jit_solution(13691983398833628721)
XLA Ops:
  0.6 66.1 %shard_map.76 = (bf16[128,4096]{1,0:T(8,128)(2,1)}, f32[32,128]{1,0:T(8,128)}, f32[256,1024]{1,0:T(8,128)}) custom-call(s32[8,32]{1,0:T(8,128)} %bitcast.7, s32[32,128]{1,0:T(8,128)} %bitcast.4, bf16[32,128]{1,0:T(8,128)(2,1)} %bitcast.6, bf16[128,4096]{1,0:T(8,128)(2,1)} %cot_ref.1, bf16[256,4096]{1,0:T(8,128)(2,1)} %values_ref.1), custom_call_target="tpu_custom_call" | custom-call | tf_op jit(solution)/shard_map/pallas_call | solution.py:319
  66.7 0.0 copy-start.1
  66.7 0.0 copy-start
  66.7 2.4 %copy.11 = bf16[128,4096]{1,0:T(8,128)(2,1)} copy(bf16[128,4096]{1,0:T(8,128)(2,1)} %get-tuple-element.12) | data formatting | bytes 2097152
  69.1 0.0 copy-done.1
  69.1 0.6 copy.12
  69.7 0.0 copy-done
  69.7 1.0 %copy.13 = f32[256,1024]{1,0:T(8,128)} copy(f32[256,1024]{1,0:T(8,128)S(1)} %copy-done) | data formatting | bytes 2097152
Async XLA Ops:
  66.7 2.4 %copy-start.1 = (f32[32,128]{1,0:T(8,128)S(1)}, f32[32,128]{1,0:T(8,128)}, u32[]{:S(2)}) copy-start(f32[32,128]{1,0:T(8,128)} %get-tuple-element.7) | copy-start | bytes 49156
  66.7 3.0 %copy-start = (f32[256,1024]{1,0:T(8,128)S(1)}, f32[256,1024]{1,0:T(8,128)}, u32[]{:S(2)}) copy-start(f32[256,1024]{1,0:T(8,128)} %get-tuple-element.14) | copy-start | bytes 3145732

commit v3 on v2

--- a/solution.py
+++ b/solution.py
@@ -9,6 +9,7 @@
 
 MESH = pl.DeviceIdType.MESH
 STEPS = 32000.0
+CHUNKS = 2
 
 
 def iota(shape, axis):
@@ -39,7 +40,7 @@
     lists_ref, pos_ref, w_ref, cot_ref, values_ref,
     out_ref, wgrad_ref, vgrad_ref,
     dense_w, step_mine, step_got, lists_got, coded_mine, coded_got, hot, vals, picked, arrived,
-    sum_mine, sum_coded, sum_got, sum_step, sum_step_got,
+    sum_mine, sum_part, sum_coded, sum_got, sum_step, sum_step_got,
     list_ss, list_rs, step_ss, step_rs, grad_ss, grad_rs, val_ss, val_rs,
     line_ss, line_rs, sum_ss, sum_rs, own_sem,
 ):
@@ -104,22 +105,25 @@
 
     pl.semaphore_wait(barrier, group - 1 + has_below.astype(jnp.int32) + has_above.astype(jnp.int32))
 
-    def line_copy(k, up):
+    wide = cols // CHUNKS
+
+    def line_copy(k, up, c):
         way = 1 if up else 0
-        return remote(
-            vals.at[k], vals.at[k], line_ss.at[way, k], line_rs.at[k], dp, mem + n_x if up else mem - n_x
-        )
-
-    def pass_on(k, up):
-        pl.when(has_above if up else has_below)(lambda: line_copy(k, up).start())
+        part = vals.at[k, :, pl.ds(c * wide, wide)]
+        to = mem + n_x if up else mem - n_x
+        return remote(part, part, line_ss.at[way, c, k], line_rs.at[c, k], dp, to)
+
+    def pass_on(k, up, c):
+        pl.when(has_above if up else has_below)(lambda: line_copy(k, up, c).start())
 
     def list_copy(d, h, g):
         return plane(lists_ref, lists_got.at[me], list_ss.at[g], list_rs.at[me], d, h)
 
     every(lambda d, h, g: list_copy(d, h, g).start())
     own.wait()
-    pass_on(z, True)
-    pass_on(z, False)
+    for c in range(CHUNKS):
+        pass_on(z, True, c)
+        pass_on(z, False, c)
 
     def grad_copy(k, d, h, g):
         return plane(
@@ -143,8 +147,8 @@
 
     lax.fori_loop(0, n_dp, terms_of, 0)
     every(lambda d, h, g: step_copy(d, h, g).start())
-    outer_first = [k for pair in zip(range(n_z), reversed(range(n_z))) for k in pair][:n_z]
-    for k in outer_first:
+    for i in range(n_z):
+        k = jnp.where(z >= n_z // 2, i, n_z - 1 - i)
         every(lambda d, h, g: grad_copy(k, d, h, g).start())
         coded_got[k, me] = coded_mine[dp, k * n_x + x]
     step_got[me] = step_mine[dp]
@@ -189,63 +193,76 @@
     )
     eye = iota((rows, rows), 0) == iota((rows, rows), 1)
 
-    def gathered(k):
+    def gather_wait(k):
         every(
             lambda d, h, g: plane(
                 coded_mine.at[0, 0], coded_got.at[k, g], grad_ss.at[k, g], grad_rs.at[k, g], d, h
             ).wait_recv()
         )
-        scaled = (hot[k].astype(jnp.float32) * along_lanes(step_got[...], k * n_x + x)).astype(jnp.bfloat16)
-        return decoded_sum(scaled, coded_got[k].reshape(slots, cols))
-
-    def sum_copies(k, up):
+
+    def scaled_hot(k):
+        return (hot[k].astype(jnp.float32) * along_lanes(step_got[...], k * n_x + x)).astype(jnp.bfloat16)
+
+    def gathered(k, scaled, c):
+        return decoded_sum(scaled, coded_got[k, :, :, c * wide : (c + 1) * wide].reshape(slots, wide))
+
+    def sum_copies(k, up, c):
         to = mem + n_x if up else mem - n_x
         at = jnp.where(k == z + 1, n_z, k) if up else k
         return (
-            remote(sum_step.at[k], sum_step_got.at[at], sum_ss.at[0, k], sum_rs.at[0, at], dp, to),
-            remote(sum_coded.at[k], sum_got.at[at], sum_ss.at[1, k], sum_rs.at[1, at], dp, to),
-        )
-
-    def received(at):
-        remote(sum_step.at[0], sum_step_got.at[at], sum_ss.at[0, 0], sum_rs.at[0, at], dp, mem).wait_recv()
-        remote(sum_coded.at[0], sum_got.at[at], sum_ss.at[1, 0], sum_rs.at[1, at], dp, mem).wait_recv()
-        scaled = jnp.where(eye, sum_step_got[at][0:1, :], 0.0).astype(jnp.bfloat16)
-        return decoded_sum(scaled, sum_got[at])
+            remote(sum_step.at[c, k], sum_step_got.at[c, at], sum_ss.at[0, c, k], sum_rs.at[0, c, at], dp, to),
+            remote(sum_coded.at[c, k], sum_got.at[c, at], sum_ss.at[1, c, k], sum_rs.at[1, c, at], dp, to),
+        )
+
+    def received(at, c):
+        for src, dst, i in ((sum_step, sum_step_got, 0), (sum_coded, sum_got, 1)):
+            remote(src.at[c, 0], dst.at[c, at], sum_ss.at[i, c, 0], sum_rs.at[i, c, at], dp, mem).wait_recv()
+        scaled = jnp.where(eye, sum_step_got[c, at][0:1, :], 0.0).astype(jnp.bfloat16)
+        return decoded_sum(scaled, sum_got[c, at])
 
     def relay(k, up, first):
-        sum_mine[...] = gathered(k)
-
-        @pl.when(jnp.logical_not(first))
-        def _():
-            sum_mine[...] += received(k)
-
-        q, step = coded(sum_mine[...])
-        sum_coded[k] = q
-        sum_step[k] = jnp.broadcast_to(
-            jnp.sum(jnp.where(eye, step, 0.0), axis=0, keepdims=True), sum_step.shape[1:]
-        )
-        for copy in sum_copies(k, up):
-            copy.start()
-
-    def take(k, up):
-        line_copy(k, up).wait_recv()
-        pass_on(k, up)
-        select(k)
-
-    def step_along(s, c):
+        gather_wait(k)
+        scaled = scaled_hot(k)
+        for c in range(CHUNKS):
+            sum_part[...] = gathered(k, scaled, c)
+
+            @pl.when(jnp.logical_not(first))
+            def _():
+                sum_part[...] += received(k, c)
+
+            q, step = coded(sum_part[...])
+            sum_coded[c, k] = q
+            sum_step[c, k] = jnp.broadcast_to(
+                jnp.sum(jnp.where(eye, step, 0.0), axis=0, keepdims=True), sum_step.shape[2:]
+            )
+            for copy in sum_copies(k, up, c):
+                copy.start()
+
+    def take(k, up, c):
+        line_copy(k, up, c).wait_recv()
+        pass_on(k, up, c)
+
+    def step_along(s, carry):
         @pl.when(s > 0)
         def _():
-            pl.when(z - s >= 0)(lambda: take(z - s, True))
-            pl.when(z + s < n_z)(lambda: take(z + s, False))
+            from_below, from_above = z - s >= 0, z + s < n_z
+            for c in range(CHUNKS):
+                pl.when(from_below)(lambda: take(z - s, True, c))
+                pl.when(from_above)(lambda: take(z + s, False, c))
+            pl.when(from_below)(lambda: select(z - s))
+            pl.when(from_above)(lambda: select(z + s))
 
         down = s - (n_z - 1 - z)
         pl.when((down >= 0) & (down < z))(lambda: relay(down, False, z == n_z - 1))
         up = n_z - 1 - s + z
         pl.when((up > z) & (up < n_z))(lambda: relay(up, True, z == 0))
-        return c
+        return carry
 
     lax.fori_loop(0, n_z, step_along, 0)
-    sum_mine[...] = gathered(z)
+    gather_wait(z)
+    own_hot = scaled_hot(z)
+    for c in range(CHUNKS):
+        sum_mine[:, c * wide : (c + 1) * wide] = gathered(z, own_hot, c)
 
     def val_wait(k, d, h, g):
         cols_d = pl.ds(pl.multiple_of(d * cols, cols), cols)
@@ -272,34 +289,44 @@
             jnp.where(pos_ref[k : k + 1, :] == place_of, scores, 0.0), axis=0, keepdims=True
         )
 
-    @pl.when(has_above)
-    def _():
-        sum_mine[...] += received(z)
-
-    @pl.when(has_below)
-    def _():
-        sum_mine[...] += received(n_z)
-
-    vgrad_ref[...] = sum_mine[...]
-
     every(lambda d, h, g: list_copy(d, h, g).wait_send())
     every(lambda d, h, g: step_copy(d, h, g).wait_send())
 
-    def sent(k, c):
+    def sent(k, carry):
         every(lambda d, h, g: grad_copy(k, d, h, g).wait_send())
         every(lambda d, h, g: val_copy(k, d, h, g).wait_send())
         for up in (False, True):
-            pl.when((has_above & (k <= z)) if up else (has_below & (k >= z)))(
-                lambda: line_copy(k, up).wait_send()
-            )
-
+            @pl.when((has_above & (k <= z)) if up else (has_below & (k >= z)))
+            def _():
+                for c in range(CHUNKS):
+                    line_copy(k, up, c).wait_send()
+        return carry
+
+    lax.fori_loop(0, n_z, sent, 0)
+
+    for c in range(CHUNKS):
+        at = slice(c * wide, (c + 1) * wide)
+
+        @pl.when(has_above)
+        def _():
+            sum_mine[:, at] += received(z, c)
+
+        @pl.when(has_below)
+        def _():
+            sum_mine[:, at] += received(n_z, c)
+
+        vgrad_ref[:, at] = sum_mine[:, at]
+
+    def sums_sent(k, carry):
+        for up in (False, True):
             @pl.when((k > z) if up else (k < z))
             def _():
-                for copy in sum_copies(k, up):
-                    copy.wait_send()
-        return c
-
-    lax.fori_loop(0, n_z, sent, 0)
+                for c in range(CHUNKS):
+                    for copy in sum_copies(k, up, c):
+                        copy.wait_send()
+        return carry
+
+    lax.fori_loop(0, n_z, sums_sent, 0)
 
 
 def on_device(n_dp, n_mem, slot_weight, slot_pos, touched, values, cotangent):
@@ -337,16 +364,17 @@
             pltpu.VMEM((n_z, group, cap, cols), bf16),
             pltpu.VMEM((n_mem, cap, width), bf16),
             pltpu.VMEM((rows, cols), f32),
-            pltpu.VMEM((n_z, rows, cols), i16),
-            pltpu.VMEM((n_z + 1, rows, cols), i16),
-            pltpu.VMEM((n_z, 8, rows), f32),
-            pltpu.VMEM((n_z + 1, 8, rows), f32),
+            pltpu.VMEM((rows, cols // CHUNKS), f32),
+            pltpu.VMEM((CHUNKS, n_z, rows, cols // CHUNKS), i16),
+            pltpu.VMEM((CHUNKS, n_z + 1, rows, cols // CHUNKS), i16),
+            pltpu.VMEM((CHUNKS, n_z, 8, rows), f32),
+            pltpu.VMEM((CHUNKS, n_z + 1, 8, rows), f32),
             dma((group,)), dma((group,)),
             dma((group,)), dma((group,)),
             dma((n_z, group)), dma((n_z, group)),
             dma((n_z, group)), dma((n_z, group)),
-            dma((2, n_z)), dma((n_z,)),
-            dma((2, n_z)), dma((2, n_z + 1)),
+            dma((2, CHUNKS, n_z)), dma((CHUNKS, n_z)),
+            dma((2, CHUNKS, n_z)), dma((2, CHUNKS, n_z + 1)),
             dma,
         ],
         compiler_params=pltpu.CompilerParams(

time: 70.9 us -> 66.7 us (0.941)
  Pallas kernels: 66.1 us -> 61.8 us
    pallas_call x1, Pallas kernels: 66.1 us -> 61.8 us  [on_device(): pl.pallas_call(functools.partial(kernel, n_dp, n_mem, n_x), out_shape=(ja...]
where the time goes in v3:
time: 66.7 us; the launch traced here: 66.5 us
  Pallas kernels  61.8 us (93%)
  local copies, waits for them, and re-layouts  3.96 us (6%)
    pallas_call x1, Pallas kernels, on_device(): pl.pallas_call(functools.partial(kernel, n_dp, n_mem, n_x), out_shape=(ja...  61.8 us
    unnamed x7, local copies, waits for them, and re-layouts  3.96 us

profile of v3, /device:TPU:0, one launch (start us, length us, event | category | flops | bytes accessed | tf_op | source)
XLA Modules:
  0.0 66.5 jit_solution(9381210106285202742)
XLA Ops:
  0.6 61.8 %shard_map.76 = (bf16[128,4096]{1,0:T(8,128)(2,1)}, f32[32,128]{1,0:T(8,128)}, f32[256,1024]{1,0:T(8,128)}) custom-call(s32[8,32]{1,0:T(8,128)} %bitcast.7, s32[32,128]{1,0:T(8,128)} %bitcast.4, bf16[32,128]{1,0:T(8,128)(2,1)} %bitcast.6, bf16[128,4096]{1,0:T(8,128)(2,1)} %cot_ref.1, bf16[256,4096]{1,0:T(8,128)(2,1)} %values_ref.1), custom_call_target="tpu_custom_call" | custom-call | tf_op jit(solution)/shard_map/pallas_call | solution.py:346
  62.5 0.0 copy-start.1
  62.5 0.0 copy-start
  62.5 2.4 %copy.11 = bf16[128,4096]{1,0:T(8,128)(2,1)} copy(bf16[128,4096]{1,0:T(8,128)(2,1)} %get-tuple-element.12) | data formatting | bytes 2097152
  64.9 0.0 copy-done.1
  64.9 0.6 copy.12
  65.5 0.0 copy-done
  65.5 1.0 %copy.13 = f32[256,1024]{1,0:T(8,128)} copy(f32[256,1024]{1,0:T(8,128)S(1)} %copy-done) | data formatting | bytes 2097152
Async XLA Ops:
  62.5 2.4 %copy-start.1 = (f32[32,128]{1,0:T(8,128)S(1)}, f32[32,128]{1,0:T(8,128)}, u32[]{:S(2)}) copy-start(f32[32,128]{1,0:T(8,128)} %get-tuple-element.7) | copy-start | bytes 49156
  62.5 3.0 %copy-start = (f32[256,1024]{1,0:T(8,128)S(1)}, f32[256,1024]{1,0:T(8,128)}, u32[]{:S(2)}) copy-start(f32[256,1024]{1,0:T(8,128)} %get-tuple-element.14) | copy-start | bytes 3145732

commit v4 on v3

--- a/solution.py
+++ b/solution.py
@@ -64,11 +64,24 @@
         h = lax.rem(x + 1 + lax.rem(t, n_x), n_x)
         return d, h, d * n_x + h
 
+    places = [place(t) for t in range(group - 1)] if group <= 8 else None
+
     def every(fn):
+        if places is not None:
+            for spot in places:
+                fn(*spot)
+            return
+
         def body(t, c):
             fn(*place(t))
             return c
         lax.fori_loop(0, group - 1, body, 0)
+
+    def all_sent(like, sem):
+        plane(like, like, sem, sem, dp, x).wait_send()
+
+    def all_here(like, sem):
+        plane(like, like, sem, sem, dp, x).wait_recv()
 
     def remote(src, dst, ss, rs, d, m):
         return pltpu.make_async_remote_copy(
@@ -117,7 +130,7 @@
         pl.when(has_above if up else has_below)(lambda: line_copy(k, up, c).start())
 
     def list_copy(d, h, g):
-        return plane(lists_ref, lists_got.at[me], list_ss.at[g], list_rs.at[me], d, h)
+        return plane(lists_ref, lists_got.at[me], list_ss.at[0], list_rs.at[0], d, h)
 
     every(lambda d, h, g: list_copy(d, h, g).start())
     own.wait()
@@ -127,33 +140,39 @@
 
     def grad_copy(k, d, h, g):
         return plane(
-            coded_mine.at[d, k * n_x + h], coded_got.at[k, me], grad_ss.at[k, g], grad_rs.at[k, me], d, h
+            coded_mine.at[k, d, h], coded_got.at[k, me], grad_ss.at[k], grad_rs.at[k], d, h
         )
 
     def step_copy(d, h, g):
-        return plane(step_mine.at[d], step_got.at[me], step_ss.at[g], step_rs.at[me], d, h)
-
-    to_owner = (iota((n_mem, spread), 1) >> bits == iota((n_mem, spread), 0)).astype(jnp.bfloat16)
-    to_lane = iota((spread, cap), 0) & (cap - 1) == iota((spread, cap), 1)
-
-    def terms_of(d, c):
-        block = cot_ref[:, pl.ds(pl.multiple_of(d * cols, cols), cols)]
-        q, step = coded(jnp.dot(dense_w[...], block, preferred_element_type=jnp.float32))
-        coded_mine[d] = q.reshape(n_mem, cap, cols)
-        step_mine[d] = jnp.dot(
-            to_owner, jnp.where(to_lane, step, 0.0).astype(jnp.bfloat16), preferred_element_type=jnp.float32
-        )
-        return c
-
-    lax.fori_loop(0, n_dp, terms_of, 0)
-    every(lambda d, h, g: step_copy(d, h, g).start())
+        return plane(step_mine.at[d], step_got.at[me], step_ss.at[0], step_rs.at[0], d, h)
+
+    part = n_x * cap
+    to_lane = iota((part, cap), 0) & (cap - 1) == iota((part, cap), 1)
+    steps = [jnp.zeros((n_mem, cap), jnp.float32) for _ in range(n_dp)]
     for i in range(n_z):
         k = jnp.where(z >= n_z // 2, i, n_z - 1 - i)
+        weights_k = dense_w[pl.ds(pl.multiple_of(k * part, part), part), :]
+        to_owner = iota((n_mem, part), 0) == (iota((n_mem, part), 1) >> bits) + k * n_x
+        for d in range(n_dp):
+            q, step = coded(
+                jnp.dot(weights_k, cot_ref[:, d * cols : (d + 1) * cols], preferred_element_type=jnp.float32)
+            )
+            coded_mine[k, d] = q.reshape(n_x, cap, cols)
+            steps[d] += jnp.dot(
+                to_owner.astype(jnp.bfloat16),
+                jnp.where(to_lane, step, 0.0).astype(jnp.bfloat16),
+                preferred_element_type=jnp.float32,
+            )
         every(lambda d, h, g: grad_copy(k, d, h, g).start())
-        coded_got[k, me] = coded_mine[dp, k * n_x + x]
+    for d in range(n_dp):
+        step_mine[d] = steps[d]
+    every(lambda d, h, g: step_copy(d, h, g).start())
     step_got[me] = step_mine[dp]
-
-    every(lambda d, h, g: plane(lists_ref, lists_got.at[g], list_ss.at[g], list_rs.at[g], d, h).wait_recv())
+    for k in range(n_z):
+        coded_got[k, me] = coded_mine[k, dp, x]
+
+    others = pl.ds(0, group - 1)
+    all_here(lists_got.at[others], list_rs.at[0])
     slots = group * cap
     fan = (iota((cap, slots), 1) & (cap - 1) == iota((cap, slots), 0)).astype(jnp.bfloat16)
     diag = iota((group, slots), 1) >> bits == iota((group, slots), 0)
@@ -175,7 +194,7 @@
 
     def val_copy(k, d, h, g):
         return plane(
-            picked.at[k, g], arrived.at[k * n_x + x, :, my_cols], val_ss.at[k, g], val_rs.at[k, me], d, h
+            picked.at[k, g], arrived.at[k * n_x + x, :, my_cols], val_ss.at[k], val_rs.at[k], d, h
         )
 
     def select(k):
@@ -188,17 +207,11 @@
 
     select(z)
 
-    every(
-        lambda d, h, g: plane(step_mine.at[0], step_got.at[g], step_ss.at[g], step_rs.at[g], d, h).wait_recv()
-    )
+    all_here(step_got.at[others], step_rs.at[0])
     eye = iota((rows, rows), 0) == iota((rows, rows), 1)
 
     def gather_wait(k):
-        every(
-            lambda d, h, g: plane(
-                coded_mine.at[0, 0], coded_got.at[k, g], grad_ss.at[k, g], grad_rs.at[k, g], d, h
-            ).wait_recv()
-        )
+        all_here(coded_got.at[k, others], grad_rs.at[k])
 
     def scaled_hot(k):
         return (hot[k].astype(jnp.float32) * along_lanes(step_got[...], k * n_x + x)).astype(jnp.bfloat16)
@@ -264,14 +277,8 @@
     for c in range(CHUNKS):
         sum_mine[:, c * wide : (c + 1) * wide] = gathered(z, own_hot, c)
 
-    def val_wait(k, d, h, g):
-        cols_d = pl.ds(pl.multiple_of(d * cols, cols), cols)
-        plane(
-            picked.at[k, g], arrived.at[k * n_x + h, :, cols_d], val_ss.at[k, g], val_rs.at[k, g], d, h
-        ).wait_recv()
-
     for k in range(n_z):
-        every(lambda d, h, g: val_wait(k, d, h, g))
+        all_here(picked.at[k, others], val_rs.at[k])
 
     def tokens(b, scores):
         at = pl.ds(pl.multiple_of(b * cols, cols), cols)
@@ -289,12 +296,12 @@
             jnp.where(pos_ref[k : k + 1, :] == place_of, scores, 0.0), axis=0, keepdims=True
         )
 
-    every(lambda d, h, g: list_copy(d, h, g).wait_send())
-    every(lambda d, h, g: step_copy(d, h, g).wait_send())
+    all_sent(lists_got.at[others], list_ss.at[0])
+    all_sent(step_got.at[others], step_ss.at[0])
 
     def sent(k, carry):
-        every(lambda d, h, g: grad_copy(k, d, h, g).wait_send())
-        every(lambda d, h, g: val_copy(k, d, h, g).wait_send())
+        all_sent(coded_got.at[k, others], grad_ss.at[k])
+        all_sent(picked.at[k, others], val_ss.at[k])
         for up in (False, True):
             @pl.when((has_above & (k <= z)) if up else (has_below & (k >= z)))
             def _():
@@ -357,7 +364,7 @@
             pltpu.VMEM((n_dp, n_mem, cap), f32),
             pltpu.VMEM((group, n_mem, cap), f32),
             pltpu.VMEM((group, n_mem, cap), jnp.int32),
-            pltpu.VMEM((n_dp, n_mem, cap, cols), i16),
+            pltpu.VMEM((n_z, n_dp, n_x, cap, cols), i16),
             pltpu.VMEM((n_z, group, cap, cols), i16),
             pltpu.VMEM((n_z, rows, group * cap), bf16),
             pltpu.VMEM((n_z, rows, cols), bf16),
@@ -369,10 +376,10 @@
             pltpu.VMEM((CHUNKS, n_z + 1, rows, cols // CHUNKS), i16),
             pltpu.VMEM((CHUNKS, n_z, 8, rows), f32),
             pltpu.VMEM((CHUNKS, n_z + 1, 8, rows), f32),
-            dma((group,)), dma((group,)),
-            dma((group,)), dma((group,)),
-            dma((n_z, group)), dma((n_z, group)),
-            dma((n_z, group)), dma((n_z, group)),
+            dma((1,)), dma((1,)),
+            dma((1,)), dma((1,)),
+            dma((n_z,)), dma((n_z,)),
+            dma((n_z,)), dma((n_z,)),
             dma((2, CHUNKS, n_z)), dma((CHUNKS, n_z)),
             dma((2, CHUNKS, n_z)), dma((2, CHUNKS, n_z + 1)),
             dma,

time: 66.7 us -> 77.8 us (1.17)
  Pallas kernels: 61.8 us -> 72.9 us
    pallas_call x1, Pallas kernels: 61.8 us -> 72.9 us  [on_device(): pl.pallas_call(functools.partial(kernel, n_dp, n_mem, n_x), out_shape=(ja...]
where the time goes in v4:
time: 77.8 us; the launch traced here: 77.5 us
  Pallas kernels  72.9 us (94%)
  local copies, waits for them, and re-layouts  3.96 us (5%)
    pallas_call x1, Pallas kernels, on_device(): pl.pallas_call(functools.partial(kernel, n_dp, n_mem, n_x), out_shape=(ja...  72.9 us
    unnamed x7, local copies, waits for them, and re-layouts  3.96 us

profile of v4, /device:TPU:0, one launch (start us, length us, event | category | flops | bytes accessed | tf_op | source)
XLA Modules:
  0.0 77.5 jit_solution(2610174560653514699)
XLA Ops:
  0.6 72.9 %shard_map.76 = (bf16[128,4096]{1,0:T(8,128)(2,1)}, f32[32,128]{1,0:T(8,128)}, f32[256,1024]{1,0:T(8,128)}) custom-call(s32[8,32]{1,0:T(8,128)} %bitcast.7, s32[32,128]{1,0:T(8,128)} %bitcast.4, bf16[32,128]{1,0:T(8,128)(2,1)} %bitcast.6, bf16[128,4096]{1,0:T(8,128)(2,1)} %cot_ref.1, bf16[256,4096]{1,0:T(8,128)(2,1)} %values_ref.1), custom_call_target="tpu_custom_call" | custom-call | tf_op jit(solution)/shard_map/pallas_call | solution.py:353
  73.5 0.0 copy-start.1
  73.6 0.0 copy-start
  73.6 2.4 %copy.11 = bf16[128,4096]{1,0:T(8,128)(2,1)} copy(bf16[128,4096]{1,0:T(8,128)(2,1)} %get-tuple-element.12) | data formatting | bytes 2097152
  75.9 0.0 copy-done.1
  75.9 0.6 copy.12
  76.5 0.0 copy-done
  76.6 1.0 %copy.13 = f32[256,1024]{1,0:T(8,128)} copy(f32[256,1024]{1,0:T(8,128)S(1)} %copy-done) | data formatting | bytes 2097152
Async XLA Ops:
  73.5 2.4 %copy-start.1 = (f32[32,128]{1,0:T(8,128)S(1)}, f32[32,128]{1,0:T(8,128)}, u32[]{:S(2)}) copy-start(f32[32,128]{1,0:T(8,128)} %get-tuple-element.7) | copy-start | bytes 49156
  73.6 3.0 %copy-start = (f32[256,1024]{1,0:T(8,128)S(1)}, f32[256,1024]{1,0:T(8,128)}, u32[]{:S(2)}) copy-start(f32[256,1024]{1,0:T(8,128)} %get-tuple-element.14) | copy-start | bytes 3145732

commit v5 on v4

--- a/solution.py
+++ b/solution.py
@@ -143,12 +143,11 @@
             coded_mine.at[k, d, h], coded_got.at[k, me], grad_ss.at[k], grad_rs.at[k], d, h
         )
 
-    def step_copy(d, h, g):
-        return plane(step_mine.at[d], step_got.at[me], step_ss.at[0], step_rs.at[0], d, h)
+    def step_copy(k, d, h, g):
+        return plane(step_mine.at[k, d], step_got.at[k, me], step_ss.at[k], step_rs.at[k], d, h)
 
     part = n_x * cap
     to_lane = iota((part, cap), 0) & (cap - 1) == iota((part, cap), 1)
-    steps = [jnp.zeros((n_mem, cap), jnp.float32) for _ in range(n_dp)]
     for i in range(n_z):
         k = jnp.where(z >= n_z // 2, i, n_z - 1 - i)
         weights_k = dense_w[pl.ds(pl.multiple_of(k * part, part), part), :]
@@ -158,17 +157,15 @@
                 jnp.dot(weights_k, cot_ref[:, d * cols : (d + 1) * cols], preferred_element_type=jnp.float32)
             )
             coded_mine[k, d] = q.reshape(n_x, cap, cols)
-            steps[d] += jnp.dot(
+            step_mine[k, d] = jnp.dot(
                 to_owner.astype(jnp.bfloat16),
                 jnp.where(to_lane, step, 0.0).astype(jnp.bfloat16),
                 preferred_element_type=jnp.float32,
             )
+        every(lambda d, h, g: step_copy(k, d, h, g).start())
         every(lambda d, h, g: grad_copy(k, d, h, g).start())
-    for d in range(n_dp):
-        step_mine[d] = steps[d]
-    every(lambda d, h, g: step_copy(d, h, g).start())
-    step_got[me] = step_mine[dp]
     for k in range(n_z):
+        step_got[k, me] = step_mine[k, dp]
         coded_got[k, me] = coded_mine[k, dp, x]
 
     others = pl.ds(0, group - 1)
@@ -207,14 +204,14 @@
 
     select(z)
 
-    all_here(step_got.at[others], step_rs.at[0])
     eye = iota((rows, rows), 0) == iota((rows, rows), 1)
 
     def gather_wait(k):
+        all_here(step_got.at[k, others], step_rs.at[k])
         all_here(coded_got.at[k, others], grad_rs.at[k])
 
     def scaled_hot(k):
-        return (hot[k].astype(jnp.float32) * along_lanes(step_got[...], k * n_x + x)).astype(jnp.bfloat16)
+        return (hot[k].astype(jnp.float32) * along_lanes(step_got[k], k * n_x + x)).astype(jnp.bfloat16)
 
     def gathered(k, scaled, c):
         return decoded_sum(scaled, coded_got[k, :, :, c * wide : (c + 1) * wide].reshape(slots, wide))
@@ -297,9 +294,9 @@
         )
 
     all_sent(lists_got.at[others], list_ss.at[0])
-    all_sent(step_got.at[others], step_ss.at[0])
 
     def sent(k, carry):
+        all_sent(step_got.at[k, others], step_ss.at[k])
         all_sent(coded_got.at[k, others], grad_ss.at[k])
         all_sent(picked.at[k, others], val_ss.at[k])
         for up in (False, True):
@@ -361,8 +358,8 @@
         out_specs=(vmem, vmem, vmem),
         scratch_shapes=[
             pltpu.VMEM((n_mem * cap, toks), bf16),
-            pltpu.VMEM((n_dp, n_mem, cap), f32),
-            pltpu.VMEM((group, n_mem, cap), f32),
+            pltpu.VMEM((n_z, n_dp, n_mem, cap), f32),
+            pltpu.VMEM((n_z, group, n_mem, cap), f32),
             pltpu.VMEM((group, n_mem, cap), jnp.int32),
             pltpu.VMEM((n_z, n_dp, n_x, cap, cols), i16),
             pltpu.VMEM((n_z, group, cap, cols), i16),
@@ -377,7 +374,7 @@
             pltpu.VMEM((CHUNKS, n_z, 8, rows), f32),
             pltpu.VMEM((CHUNKS, n_z + 1, 8, rows), f32),
             dma((1,)), dma((1,)),
-            dma((1,)), dma((1,)),
+            dma((n_z,)), dma((n_z,)),
             dma((n_z,)), dma((n_z,)),
             dma((n_z,)), dma((n_z,)),
             dma((2, CHUNKS, n_z)), dma((CHUNKS, n_z)),

time: 77.8 us -> 64.4 us (0.83)
  Pallas kernels: 72.9 us -> 59.5 us
    pallas_call x1, Pallas kernels: 72.9 us -> 59.5 us  [on_device(): pl.pallas_call(functools.partial(kernel, n_dp, n_mem, n_x), out_shape=(ja...]
where the time goes in v5:
time: 64.4 us; the launch traced here: 64.1 us
  Pallas kernels  59.5 us (92%)
  local copies, waits for them, and re-layouts  3.96 us (6%)
  between operations  0.66 us (1%)
    pallas_call x1, Pallas kernels, on_device(): pl.pallas_call(functools.partial(kernel, n_dp, n_mem, n_x), out_shape=(ja...  59.5 us
    unnamed x7, local copies, waits for them, and re-layouts  3.96 us

profile of v5, /device:TPU:0, one launch (start us, length us, event | category | flops | bytes accessed | tf_op | source)
XLA Modules:
  0.0 64.1 jit_solution(9334839453202605032)
XLA Ops:
  0.6 59.5 %shard_map.76 = (bf16[128,4096]{1,0:T(8,128)(2,1)}, f32[32,128]{1,0:T(8,128)}, f32[256,1024]{1,0:T(8,128)}) custom-call(s32[8,32]{1,0:T(8,128)} %bitcast.7, s32[32,128]{1,0:T(8,128)} %bitcast.4, bf16[32,128]{1,0:T(8,128)(2,1)} %bitcast.6, bf16[128,4096]{1,0:T(8,128)(2,1)} %cot_ref.1, bf16[256,4096]{1,0:T(8,128)(2,1)} %values_ref.1), custom_call_target="tpu_custom_call" | custom-call | tf_op jit(solution)/shard_map/pallas_call | solution.py:350
  60.2 0.0 copy-start.1
  60.2 0.0 copy-start
  60.2 2.4 %copy.11 = bf16[128,4096]{1,0:T(8,128)(2,1)} copy(bf16[128,4096]{1,0:T(8,128)(2,1)} %get-tuple-element.12) | data formatting | bytes 2097152
  62.6 0.0 copy-done.1
  62.6 0.6 copy.12
  63.2 0.0 copy-done
  63.2 1.0 %copy.13 = f32[256,1024]{1,0:T(8,128)} copy(f32[256,1024]{1,0:T(8,128)S(1)} %copy-done) | data formatting | bytes 2097152
Async XLA Ops:
  60.2 2.4 %copy-start.1 = (f32[32,128]{1,0:T(8,128)S(1)}, f32[32,128]{1,0:T(8,128)}, u32[]{:S(2)}) copy-start(f32[32,128]{1,0:T(8,128)} %get-tuple-element.7) | copy-start | bytes 49156
  60.2 3.0 %copy-start = (f32[256,1024]{1,0:T(8,128)S(1)}, f32[256,1024]{1,0:T(8,128)}, u32[]{:S(2)}) copy-start(f32[256,1024]{1,0:T(8,128)} %get-tuple-element.14) | copy-start | bytes 3145732

commit v6 on v5

--- a/solution.py
+++ b/solution.py
@@ -37,9 +37,9 @@
 
 def kernel(
     n_dp, n_mem, n_x,
-    lists_ref, pos_ref, w_ref, cot_ref, values_ref,
-    out_ref, wgrad_ref, vgrad_ref,
-    dense_w, step_mine, step_got, lists_got, coded_mine, coded_got, hot, vals, picked, arrived,
+    lists_ref, pos_ref, w_ref, cot_hbm, values_ref,
+    out_hbm, wgrad_ref, vgrad_ref,
+    cot_ref, out_ref, dense_wt, dense_w, step_mine, step_got, lists_got, coded_mine, coded_got, hot, vals, picked, arrived,
     sum_mine, sum_part, sum_coded, sum_got, sum_step, sum_step_got,
     list_ss, list_rs, step_ss, step_rs, grad_ss, grad_rs, val_ss, val_rs,
     line_ss, line_rs, sum_ss, sum_rs, own_sem,
@@ -49,7 +49,7 @@
     cap = lists_ref.shape[1]
     topk, toks = pos_ref.shape
     rows = values_ref.shape[0]
-    cols = cot_ref.shape[1] // n_dp
+    cols = cot_hbm.shape[1] // n_dp
     spread = n_mem * cap
     bits = cap.bit_length() - 1
     dp = lax.axis_index("dp")
@@ -92,6 +92,8 @@
         return remote(src, dst, ss, rs, d, z * n_x + h)
 
     barrier = pltpu.get_barrier_semaphore()
+    cot_in = pltpu.make_async_copy(cot_hbm, cot_ref, own_sem.at[1])
+    cot_in.start()
 
     def greet(m):
         pl.semaphore_signal(barrier, inc=1, device_id=(dp, m), device_id_type=MESH)
@@ -105,7 +107,7 @@
     pl.when(has_above)(lambda: greet(mem + n_x))
 
     my_cols = pl.ds(pl.multiple_of(dp * cols, cols), cols)
-    own = pltpu.make_async_copy(values_ref.at[:, my_cols], vals.at[z], own_sem)
+    own = pltpu.make_async_copy(values_ref.at[:, my_cols], vals.at[z], own_sem.at[0])
     own.start()
     lists_got[me] = lists_ref[...]
 
@@ -146,6 +148,7 @@
     def step_copy(k, d, h, g):
         return plane(step_mine.at[k, d], step_got.at[k, me], step_ss.at[k], step_rs.at[k], d, h)
 
+    cot_in.wait()
     part = n_x * cap
     to_lane = iota((part, cap), 0) & (cap - 1) == iota((part, cap), 1)
     for i in range(n_z):
@@ -204,6 +207,8 @@
 
     select(z)
 
+    dense_wt[...] = dense_w[...].astype(jnp.float32).T.astype(jnp.bfloat16)
+
     eye = iota((rows, rows), 0) == iota((rows, rows), 1)
 
     def gather_wait(k):
@@ -280,14 +285,16 @@
     def tokens(b, scores):
         at = pl.ds(pl.multiple_of(b * cols, cols), cols)
         table = arrived[:, :, at].reshape(spread, cols)
-        out_ref[:, at] = lax.dot_general(
-            dense_w[...], table, (((0,), (0,)), ((), ())), preferred_element_type=jnp.float32
+        out_ref[:, at] = jnp.dot(
+            dense_wt[...], table, preferred_element_type=jnp.float32
         ).astype(out_ref.dtype)
         return scores + lax.dot_general(
             table, cot_ref[:, at], (((1,), (1,)), ((), ())), preferred_element_type=jnp.float32
         )
 
     scores = lax.fori_loop(0, n_dp, tokens, jnp.zeros((spread, toks), jnp.float32))
+    out_back = pltpu.make_async_copy(out_ref, out_hbm, own_sem.at[1])
+    out_back.start()
     for k in range(topk):
         wgrad_ref[k : k + 1, :] = jnp.sum(
             jnp.where(pos_ref[k : k + 1, :] == place_of, scores, 0.0), axis=0, keepdims=True
@@ -331,6 +338,7 @@
         return carry
 
     lax.fori_loop(0, n_z, sums_sent, 0)
+    out_back.wait()
 
 
 def on_device(n_dp, n_mem, slot_weight, slot_pos, touched, values, cotangent):
@@ -354,9 +362,12 @@
             jax.ShapeDtypeStruct((topk, toks), f32),
             jax.ShapeDtypeStruct((rows, cols), f32),
         ),
-        in_specs=[vmem, vmem, vmem, vmem, pl.BlockSpec(memory_space=pl.ANY)],
-        out_specs=(vmem, vmem, vmem),
+        in_specs=[vmem, vmem, vmem, pl.BlockSpec(memory_space=pl.ANY), pl.BlockSpec(memory_space=pl.ANY)],
+        out_specs=(pl.BlockSpec(memory_space=pl.ANY), vmem, vmem),
         scratch_shapes=[
+            pltpu.VMEM((toks, width), bf16),
+            pltpu.VMEM((toks, width), bf16),
+            pltpu.VMEM((toks, n_mem * cap), bf16),
             pltpu.VMEM((n_mem * cap, toks), bf16),
             pltpu.VMEM((n_z, n_dp, n_mem, cap), f32),
             pltpu.VMEM((n_z, group, n_mem, cap), f32),
@@ -379,7 +390,7 @@
             dma((n_z,)), dma((n_z,)),
             dma((2, CHUNKS, n_z)), dma((CHUNKS, n_z)),
             dma((2, CHUNKS, n_z)), dma((2, CHUNKS, n_z + 1)),
-            dma,
+            dma((2,)),
         ],
         compiler_params=pltpu.CompilerParams(
             collective_id=0, has_side_effects=True, vmem_limit_bytes=60 * 2**20

time: 64.4 us -> 63.5 us (0.986)
  Pallas kernels: 59.5 us -> 58.6 us
    pallas_call x1, Pallas kernels: 59.5 us -> 58.6 us  [on_device(): pl.pallas_call(functools.partial(kernel, n_dp, n_mem, n_x), out_shape=(ja...]
where the time goes in v6:
time: 63.5 us; the launch traced here: 63.2 us
  Pallas kernels  58.6 us (92%)
  local copies, waits for them, and re-layouts  3.96 us (6%)
  between operations  0.66 us (1%)
    pallas_call x1, Pallas kernels, on_device(): pl.pallas_call(functools.partial(kernel, n_dp, n_mem, n_x), out_shape=(ja...  58.6 us
    unnamed x7, local copies, waits for them, and re-layouts  3.96 us

profile of v6, /device:TPU:0, one launch (start us, length us, event | category | flops | bytes accessed | tf_op | source)
XLA Modules:
  0.0 63.2 jit_solution(4916358164777491619)
XLA Ops:
  0.6 58.6 %shard_map.76 = (bf16[128,4096]{1,0:T(8,128)(2,1)}, f32[32,128]{1,0:T(8,128)}, f32[256,1024]{1,0:T(8,128)}) custom-call(s32[8,32]{1,0:T(8,128)} %bitcast.7, s32[32,128]{1,0:T(8,128)} %bitcast.4, bf16[32,128]{1,0:T(8,128)(2,1)} %bitcast.6, bf16[128,4096]{1,0:T(8,128)(2,1)} %cot_hbm.1, bf16[256,4096]{1,0:T(8,128)(2,1)} %values_ref.1), custom_call_target="tpu_custom_call" | custom-call | tf_op jit(solution)/shard_map/pallas_call | solution.py:358
  59.2 0.0 copy-start.1
  59.2 0.0 copy-start
  59.3 2.4 %copy.11 = bf16[128,4096]{1,0:T(8,128)(2,1)} copy(bf16[128,4096]{1,0:T(8,128)(2,1)} %get-tuple-element.12) | data formatting | bytes 2097152
  61.6 0.0 copy-done.1
  61.6 0.6 copy.12
  62.2 0.0 copy-done
  62.2 1.0 %copy.13 = f32[256,1024]{1,0:T(8,128)} copy(f32[256,1024]{1,0:T(8,128)S(1)} %copy-done) | data formatting | bytes 2097152
Async XLA Ops:
  59.2 2.4 %copy-start.1 = (f32[32,128]{1,0:T(8,128)S(1)}, f32[32,128]{1,0:T(8,128)}, u32[]{:S(2)}) copy-start(f32[32,128]{1,0:T(8,128)} %get-tuple-element.7) | copy-start | bytes 49156
  59.2 3.0 %copy-start = (f32[256,1024]{1,0:T(8,128)S(1)}, f32[256,1024]{1,0:T(8,128)}, u32[]{:S(2)}) copy-start(f32[256,1024]{1,0:T(8,128)} %get-tuple-element.14) | copy-start | bytes 3145732

commit v7 on v6

--- a/solution.py
+++ b/solution.py
@@ -9,7 +9,7 @@
 
 MESH = pl.DeviceIdType.MESH
 STEPS = 32000.0
-CHUNKS = 2
+CHUNKS = 4
 
 
 def iota(shape, axis):

time: 63.5 us -> 64.4 us (1.014)
  Pallas kernels: 58.6 us -> 59.5 us
    pallas_call x1, Pallas kernels: 58.6 us -> 59.5 us  [on_device(): pl.pallas_call(functools.partial(kernel, n_dp, n_mem, n_x), out_shape=(ja...]
where the time goes in v7:
time: 64.4 us; the launch traced here: 64.1 us
  Pallas kernels  59.5 us (92%)
  local copies, waits for them, and re-layouts  3.96 us (6%)
  between operations  0.66 us (1%)
    pallas_call x1, Pallas kernels, on_device(): pl.pallas_call(functools.partial(kernel, n_dp, n_mem, n_x), out_shape=(ja...  59.5 us
    unnamed x7, local copies, waits for them, and re-layouts  3.96 us

profile of v7, /device:TPU:0, one launch (start us, length us, event | category | flops | bytes accessed | tf_op | source)
XLA Modules:
  0.0 64.1 jit_solution(7452047968430690705)
XLA Ops:
  0.6 59.5 %shard_map.76 = (bf16[128,4096]{1,0:T(8,128)(2,1)}, f32[32,128]{1,0:T(8,128)}, f32[256,1024]{1,0:T(8,128)}) custom-call(s32[8,32]{1,0:T(8,128)} %bitcast.7, s32[32,128]{1,0:T(8,128)} %bitcast.4, bf16[32,128]{1,0:T(8,128)(2,1)} %bitcast.6, bf16[128,4096]{1,0:T(8,128)(2,1)} %cot_hbm.1, bf16[256,4096]{1,0:T(8,128)(2,1)} %values_ref.1), custom_call_target="tpu_custom_call" | custom-call | tf_op jit(solution)/shard_map/pallas_call | solution.py:358
  60.1 0.0 copy-start.1
  60.1 0.0 copy-start
  60.1 2.4 %copy.11 = bf16[128,4096]{1,0:T(8,128)(2,1)} copy(bf16[128,4096]{1,0:T(8,128)(2,1)} %get-tuple-element.12) | data formatting | bytes 2097152
  62.5 0.0 copy-done.1
  62.5 0.6 copy.12
  63.1 0.0 copy-done
  63.1 1.0 %copy.13 = f32[256,1024]{1,0:T(8,128)} copy(f32[256,1024]{1,0:T(8,128)S(1)} %copy-done) | data formatting | bytes 2097152
Async XLA Ops:
  60.1 2.4 %copy-start.1 = (f32[32,128]{1,0:T(8,128)S(1)}, f32[32,128]{1,0:T(8,128)}, u32[]{:S(2)}) copy-start(f32[32,128]{1,0:T(8,128)} %get-tuple-element.7) | copy-start | bytes 49156
  60.1 3.0 %copy-start = (f32[256,1024]{1,0:T(8,128)S(1)}, f32[256,1024]{1,0:T(8,128)}, u32[]{:S(2)}) copy-start(f32[256,1024]{1,0:T(8,128)} %get-tuple-element.14) | copy-start | bytes 3145732
